TPU v7x, 32 devices: a whole 2x2x4 slice. The times are simulated.
32 devices in a mesh: dp: 16 (over z, y, x), tensor: 2 (over core).
Axes of the slice: x: 2, y: 2, z: 4, core: 2. Of those that a mesh axis runs over, the one named last changes fastest.
Arguments:
- gradient: bfloat16 [16, 256, 3584], P('dp', 'tensor'), may hold values from -84 to 84
- thresholds: int32 [16, 256, 3584], P('dp', 'tensor'), may hold values from 0 to 4095
- sign_bits: int32 [3584], replicated, may hold values 0 or 1
- levels: int32 [16], replicated, may hold values from 0 to 36, as said below
- clip_rms: float32 [1], replicated, may hold values from 0.5 to 1
Outputs:
- summed_grad: bfloat16 [256, 3584], P('tensor')
Inputs may be any that keep to these rules, and one draw needn't show every extreme that they name: levels[0] is 0, the entries rise strictly by 1 to 4 from one to the next, and levels[15] is the promised most.
All inputs are finite; a program needn't handle non-finite values.
Results may differ from a plain program's by a relative error of at most 0.0004.
Values may be sent and summed in bfloat16 or wider, within the bound.
A program may use at most 64 MiB of HBM per device.

v0:
```python
import math

import jax
import jax.numpy as jnp
from jax import lax
from jax.sharding import PartitionSpec as P

BLOCK = 128


epsilon = 1e-06
sharpness = 16.0
dither_range = 4096.0


def hadamard_matrix(size):
    position = jnp.arange(size, dtype=jnp.int32)
    parity = jnp.zeros((size, size), jnp.int32)
    for bit_index in range(size.bit_length() - 1):
        parity = parity + (position[:, None] >> bit_index & 1) * (
            position[None, :] >> bit_index & 1
        )
    return (1 - 2 * (parity % 2)).astype(jnp.float32)


def encode_units(normed, dither, table, units):
    low_level = jnp.zeros_like(normed) + table[0]
    high_level = jnp.zeros_like(normed) + table[1]
    low_unit = jnp.zeros_like(normed) + units[0]
    high_unit = jnp.zeros_like(normed) + units[1]
    for position in range(1, table.shape[0] - 1):
        above = normed >= table[position]
        low_level = jnp.where(above, table[position], low_level)
        high_level = jnp.where(above, table[position + 1], high_level)
        low_unit = jnp.where(above, units[position], low_unit)
        high_unit = jnp.where(above, units[position + 1], high_unit)
    fraction = (normed - low_level) / (high_level - low_level)
    bottom = jax.nn.sigmoid(-sharpness * dither)
    upper_end = jax.nn.sigmoid(sharpness * (1.0 - dither))
    ramp = (jax.nn.sigmoid(sharpness * (fraction - dither)) - bottom) / (upper_end - bottom)
    return low_unit + (high_unit - low_unit) * ramp


def restore_blocks(code_sum, block_scale, hadamard, top_unit, count):
    merged = (2.0 * code_sum / top_unit - count) * block_scale[:, None]
    product = jnp.dot(merged, hadamard, precision=lax.Precision.HIGHEST)
    return product * (1.0 / math.sqrt(hadamard.shape[0]))


def body(gradient, thresholds, sign_bits, levels, clip_rms):
    row_count = gradient.shape[1]
    columns = gradient.shape[2]
    block_count = columns // BLOCK
    replica_count = float(lax.axis_size("dp"))
    hadamard = hadamard_matrix(BLOCK)
    sign_flip = (1 - 2 * sign_bits).astype(jnp.float32)
    units = levels.astype(jnp.float32)
    top_unit = units[levels.shape[0] - 1]
    table = 2.0 * units / top_unit - 1.0
    signed = gradient[0] * sign_flip.astype(jnp.bfloat16)
    blocks = signed.reshape(row_count * block_count, BLOCK)
    rotated = jnp.dot(blocks, hadamard.astype(jnp.bfloat16), preferred_element_type=jnp.float32) * (
        1.0 / math.sqrt(BLOCK)
    )
    local_peak = jnp.max(jnp.abs(rotated), axis=1)
    block_scale = lax.pmax(local_peak, "dp") + epsilon
    normed = rotated / block_scale[:, None]
    dither = (
        thresholds[0].reshape(row_count * block_count, BLOCK).astype(jnp.float32) + 0.5
    ) / dither_range
    code_values = encode_units(normed, dither, table, units)
    flip_blocks = sign_flip.reshape(block_count, BLOCK)
    entries = float(row_count * lax.axis_size("tensor") * columns)
    owned_rows = row_count * block_count // lax.axis_size("dp")
    first_row = lax.axis_index("dp") * owned_rows
    owned_sum = lax.psum_scatter(code_values, "dp", scatter_dimension=0, tiled=True)
    owned_scale = lax.dynamic_slice_in_dim(block_scale, first_row, owned_rows, 0)
    block_ids = (first_row + jnp.arange(owned_rows, dtype=jnp.int32)) % block_count
    one_hot = (block_ids[:, None] == jnp.arange(block_count, dtype=jnp.int32)[None, :]).astype(
        jnp.bfloat16
    )
    owned_flip = jnp.dot(
        one_hot, flip_blocks.astype(jnp.bfloat16), preferred_element_type=jnp.float32
    )
    restored = (
        restore_blocks(owned_sum, owned_scale, hadamard, top_unit, replica_count) * owned_flip
    )
    squares = lax.psum(jnp.sum(restored * restored), ("dp", "tensor"))
    root_mean = jnp.sqrt(squares / entries + epsilon)
    factor = clip_rms[0] / jnp.maximum(root_mean, clip_rms[0])
    owned_part = (restored * factor).astype(jnp.bfloat16)
    gathered = lax.all_gather(owned_part, "dp", axis=0, tiled=True)
    return gathered.reshape(row_count, columns)


def solution(mesh):
    in_specs = (P("dp", "tensor", None), P("dp", "tensor", None), P(), P(), P())
    out_specs = P("tensor", None)
    return jax.shard_map(body, mesh=mesh, in_specs=in_specs, out_specs=out_specs, check_vma=False)
```

profile of v0, /device:TPU:0, one launch (start us, length us, event | category | flops | bytes accessed | tf_op | source)
XLA Modules:
  0.0 306.0 jit_solution(493473136276166578)
XLA Ops:
  6.5 0.0 reduce-scatter.4.cloned.1.call-start
  6.6 3.2 %fusion = (f32[1,128,3584]{2,1,0:T(8,128)}, f32[1,128,3584]{2,1,0:T(8,128)S(1)}) fusion(s32[1,128,3584]{2,1,0:T(8,128)} %param.6), kind=kLoop, calls=%fused_computation.19 | loop fusion | flops 3211264 | bytes 5505024 | tf_op jit(solution)/shard_map/div | solution.py:68
  9.8 1.3 reshape.134
  11.1 1.8 copy.11
  12.9 2.6 div.56
  15.5 0.0 copy-start
  15.5 2.8 copy.10
  18.4 0.0 copy-done
  18.4 0.0 copy-start.1
  18.4 2.1 squeeze.68
  20.4 0.0 copy-done.1
  20.4 0.0 copy-start.2
  20.4 0.1 mul.221
  20.6 1.1 mul.222
  21.7 0.0 copy-done.2
  21.7 0.7 fusion.28
  22.4 0.6 divide_add_fusion
  23.0 0.7 fusion.27
  23.7 3.3 %abs_reduce_fusion = (f32[3584]{0:T(1024)S(1)}, f32[3584,128]{0,1:T(8,128)}) fusion(s32[128]{0:T(128)S(1)} %get-tuple-element.43, s32[128]{0:T(128)S(1)} %get-tuple-element.44, s32[128]{0:T(128)S(1)} %get-tuple-element.45, s32[128]{0:T(128)S(1)} %get-tuple-element.46, s32[128]{0:T(128)S(1)} %get-tuple-element.47, s32[128]{0:T(128)S(1)} %get-tuple-element.48, ...), kind=kOutput, calls=%fused_computation.18 | convolution fusion | flops 119730688 | bytes 3687936 | tf_op jit(solution)/shard_map/dot_general | solution.py:62
  27.0 78.6 %pmax.7 = f32[3584]{0:T(1024)S(1)} all-reduce(f32[3584]{0:T(1024)S(1)} %get-tuple-element.39), channel_id=1, replica_groups=mesh['dp'=16,'tensor'=2] {'dp'}, use_global_device_ids=true, to_apply=%region_1.2 | all-reduce | flops 3584 | bytes 28672 | tf_op jit(solution)/shard_map/pmax | solution.py:66
  105.5 27.6 %multiply_add_fusion = f32[3584,128]{0,1:T(8,128)} fusion(f32[3584,128]{0,1:T(8,128)S(1)} %copy.11, f32[3584,128]{0,1:T(8,128)} %copy.10, f32[3584,128]{0,1:T(8,128)} %get-tuple-element.40, f32[]{:T(128)} %bitcast.32, f32[]{:T(128)} %bitcast.31, f32[]{:T(128)} %bitcast.1, f32[]{:T(128)} %bitcast.30, f32[]{:T(128)} %bitcast.29, f32[]{:T(128)} %bitcast.28, ...), kind=kLoop, calls=%fused_computation.2 | loop fusion | flops 41287680 | bytes 7354496 | tf_op jit(solution)/shard_map/add | solution.py:41
  133.1 2.7 copy.14
  135.8 0.0 reduce-scatter.4.cloned.1.call-update
  135.9 0.1 dynamic_slice.3
  136.6 75.1 %reduce-scatter.4.cloned.1.call-done = f32[224,128]{1,0:T(8,128)} async-done(((f32[3584,128]{1,0:T(8,128)}), f32[224,128]{1,0:T(8,128)}) %reduce-scatter.4.cloned.1.call-update) | async-done | bytes 114704
  211.8 1.0 copy.15
  212.8 1.1 convolution_multiply_fusion.2
  213.8 0.8 multiply_reduce_fusion
  214.7 37.1 %psum.7 = f32[]{:T(128)} all-reduce(f32[]{:T(128)} %get-tuple-element.41), channel_id=1, replica_groups=mesh['dp'=16,'tensor'=2] {'dp','tensor'}, use_global_device_ids=true, to_apply=%region_4.5 | all-reduce | flops 1 | bytes 8 | tf_op jit(solution)/shard_map/psum | solution.py:88
  252.5 44.7 %all_gather.3 = bf16[3584,128]{1,0:T(8,128)(2,1)S(1)} all-gather(bf16[224,128]{1,0:T(8,128)(2,1)S(1)} %multiply_convert_fusion), channel_id=1, replica_groups=mesh['dp'=16,'tensor'=2] {'dp'}, dimensions={0}, use_global_device_ids=true | all-gather | bytes 974848 | tf_op jit(solution)/shard_map/all_gather | solution.py:92
  297.2 1.9 reshape.129
  (9 shorter events, 0.1 us)
Async XLA Ops:
  6.5 205.2 %reduce-scatter.4.cloned.1.call-start = ((), (), s32[]{:S(2)}) async-start(), calls=%async_computation.1 | async-start | bytes 1949696
  15.5 2.8 copy-start
  18.4 2.1 copy-start.1
  20.4 1.3 copy-start.2
Sparse Core Ops, SparseCore 0:
  136.0 75.7 reduce-scatter.3
where the time goes:
time: 307 us; the launch traced here: 306 us
  blocking collectives  160 us (52%)
  waiting for transfers between devices  75.2 us (24%)
  other arithmetic  31.4 us (10%)
  local copies, waits for them, and re-layouts  19 us (6%)
  between operations  14.9 us (5%)
  matrix products  5.2 us (2%)
    pmax x1, blocking collectives, body(): block_scale = lax.pmax(local_peak, 'dp') + epsilon  78.6 us
    unnamed x2, waiting for transfers between devices  75.2 us
    all_gather x1, blocking collectives, body(): gathered = lax.all_gather(owned_part, 'dp', axis=0, tiled=True)  44.7 us
    psum x1, blocking collectives, body(): squares = lax.psum(jnp.sum(restored * restored), ('dp', 'tensor'))  37.1 us
    add x1, other arithmetic, encode_units(): return low_unit + (high_unit - low_unit) * ramp  27.6 us
  transfers between devices with their start and end apart: 1, of which 1 were waited for; matrix products, arithmetic and copies ran while one was open for 0% of the time, Pallas kernels for 0%

commit v1 on v0

--- a/solution.py
+++ b/solution.py
@@ -1,16 +1,20 @@
+import functools
 import math
 
 import jax
 import jax.numpy as jnp
 from jax import lax
+from jax.experimental import pallas as pl
+from jax.experimental.pallas import tpu as pltpu
 from jax.sharding import PartitionSpec as P
 
 BLOCK = 128
-
-
+MESH = pl.DeviceIdType.MESH
+CHUNK = 2
 epsilon = 1e-06
 sharpness = 16.0
 dither_range = 4096.0
+LOG2E = math.log2(math.e)
 
 
 def hadamard_matrix(size):
@@ -21,6 +25,290 @@
             position[None, :] >> bit_index & 1
         )
     return (1 - 2 * (parity % 2)).astype(jnp.float32)
+
+
+def kernel(
+    entries, grad, thr, flip, had, levels, clip, out,
+    rot, amp, peak, peak_a, peak_b, send, recv_a, part, recv_b, merged, ssq, ssq_in,
+    pk_send, pk_a, pk_b, a_send, a_recv, b_send, b_recv, q_send, q_recv, g_send, z_recv, p_recv,
+):
+    me, core = lax.axis_index("dp"), lax.axis_index("tensor")
+    x, y, z = me % 2, (me // 2) % 2, me // 4
+    blocks = rot.shape[0]
+    half = blocks // 2
+    chunks = half // CHUNK
+    count = 16.0
+    inv_root = 1.0 / math.sqrt(BLOCK)
+
+    def plane_peer(d):
+        dx, dy = d % 2, d // 2
+        return ((y + dy) % 2) * 2 + (x + dx) % 2
+
+    def z_peer(d):
+        return (z + d) % 4
+
+    def dev(zz, q, cc=None):
+        return (zz * 4 + q, core if cc is None else cc)
+
+    def remote(src, dst, ss, rs, where):
+        return pltpu.make_async_remote_copy(
+            src_ref=src, dst_ref=dst, send_sem=ss, recv_sem=rs, device_id=where, device_id_type=MESH
+        )
+
+    mine = y * 2 + x
+    others = [(d, c) for d in range(16) for c in range(2) if (d, c) != (0, 0)]
+
+    barrier = pltpu.get_barrier_semaphore()
+    for d, c in others:
+        pl.semaphore_signal(
+            barrier, inc=1, device_id=((me + d) % 16, (core + c) % 2), device_id_type=MESH
+        )
+
+    hb = had[...].astype(jnp.bfloat16)
+    peak[...] = jnp.zeros_like(peak)
+
+    def rotate(b, _):
+        cols = pl.ds(pl.multiple_of(b * BLOCK, BLOCK), BLOCK)
+        signed = grad[:, cols] * flip[pl.ds(b, 1), :].astype(jnp.bfloat16)
+        rot[b] = jnp.dot(signed, hb, preferred_element_type=jnp.float32)
+        turned = lax.dot_general(
+            hb, signed, (((0,), (1,)), ((), ())), preferred_element_type=jnp.float32
+        )
+        peak[pl.ds(b, 1), :] = jnp.max(jnp.abs(turned), axis=0, keepdims=True) * inv_root
+        return 0
+
+    lax.fori_loop(0, blocks, rotate, 0)
+
+    def amplitude(b, _):
+        cols = pl.ds(pl.multiple_of(b * BLOCK, BLOCK), BLOCK)
+        power = (thr[:, cols].astype(jnp.float32) + 0.5) * (sharpness * LOG2E / dither_range)
+        amp[b] = jnp.exp2(power)
+        return 0
+
+    pl.semaphore_wait(barrier, len(others))
+
+    copies = []
+    first = [
+        remote(peak, peak_a.at[d - 1], pk_send.at[d - 1], pk_a.at[d - 1], dev(z, plane_peer(d)))
+        for d in range(1, 4)
+    ]
+    for c in first:
+        c.start()
+    lax.fori_loop(0, half, amplitude, 0)
+    for c in first:
+        c.wait()
+    peak[...] = jnp.maximum(
+        jnp.maximum(peak[...], peak_a[0]), jnp.maximum(peak_a[1], peak_a[2])
+    )
+    second = [
+        remote(peak, peak_b.at[d - 1], pk_send.at[d + 2], pk_b.at[d - 1], dev(z_peer(d), mine))
+        for d in range(1, 4)
+    ]
+    for c in second:
+        c.start()
+    lax.fori_loop(half, blocks, amplitude, 0)
+    for c in second:
+        c.wait()
+    scale = (
+        jnp.maximum(jnp.maximum(peak[...], peak_b[0]), jnp.maximum(peak_b[1], peak_b[2])) + epsilon
+    )
+    units = [levels[p].astype(jnp.float32) for p in range(16)]
+    top = units[15]
+    packed = [units[p] + (units[p + 1] - units[p]) * 0.125 for p in range(15)]
+    half_top = 0.5 * top
+    peak_a[0] = scale
+    peak_a[1] = (half_top * inv_root) / scale
+
+    lane = lax.broadcasted_iota(jnp.int32, (BLOCK, BLOCK), 1)
+    row = lax.broadcasted_iota(jnp.int32, (BLOCK, BLOCK), 0)
+    decay = math.exp(-sharpness)
+
+    def code_of(b):
+        inverse = jnp.sum(
+            jnp.where(lane == row, peak_a[1, pl.ds(b, 1), :], 0.0), axis=1, keepdims=True
+        )
+        place = rot[b] * inverse + half_top
+        pack = jnp.zeros_like(place) + packed[0]
+        for p in range(1, 15):
+            pack = jnp.where(place >= units[p], packed[p], pack)
+        low = jnp.floor(pack)
+        gap = (pack - low) * 8.0
+        inv_gap = ((10.0 - gap) * gap - 35.0) * gap + 50.0
+        w = jnp.exp2((place - low) * inv_gap * (-sharpness * LOG2E / 24.0))
+        a = amp[b]
+        upper = (1.0 - w) * (a * (decay / (1.0 - decay)) + 1.0 / (1.0 - decay))
+        return low + gap * (upper / (1.0 + a * w))
+
+    def plane_copy(c, d):
+        return remote(
+            send.at[c, plane_peer(d)], recv_a.at[c, d - 1], a_send.at[c, d - 1],
+            a_recv.at[c, d - 1], dev(z, plane_peer(d)),
+        )
+
+    def z_copy(c, d):
+        return remote(
+            part.at[c, z_peer(d)], recv_b.at[c, d - 1], b_send.at[c, d - 1],
+            b_recv.at[c, d - 1], dev(z_peer(d), mine),
+        )
+
+    def encode_chunk(c):
+        for h in range(2):
+            def one(k, _):
+                code = code_of(h * half + c * CHUNK + k)
+                for zz in range(4):
+                    for yy in range(2):
+                        at = 16 * (2 * zz + yy)
+                        send[c, yy * 2 + h, zz, k] = code[at:at + 16]
+                return 0
+            lax.fori_loop(0, CHUNK, one, 0)
+        for d in range(1, 4):
+            plane_copy(c, d).start()
+
+    def add_plane(c):
+        for d in range(1, 4):
+            plane_copy(c, d).wait_recv()
+        part[c] = (send[c, mine] + recv_a[c, 0]) + (recv_a[c, 1] + recv_a[c, 2])
+        for d in range(1, 4):
+            z_copy(c, d).start()
+
+    for c in range(chunks):
+        encode_chunk(c)
+        if c >= 2:
+            add_plane(c - 2)
+    for c in range(max(chunks - 2, 0), chunks):
+        add_plane(c)
+
+    group = 2 * z + y
+    lane16 = lax.broadcasted_iota(jnp.int32, (16, BLOCK), 1)
+    row16 = lax.broadcasted_iota(jnp.int32, (16, BLOCK), 0)
+    own_rows = lane16 == row16 + 16 * group
+    total = jnp.zeros((16, BLOCK), jnp.float32)
+    for c in range(chunks):
+        for d in range(1, 4):
+            z_copy(c, d).wait_recv()
+        sums = (part[c, z] + recv_b[c, 0]) + (recv_b[c, 1] + recv_b[c, 2])
+        for k in range(CHUNK):
+            b = x * half + c * CHUNK + k
+            own_scale = jnp.sum(
+                jnp.where(own_rows, peak_a[0, pl.ds(b, 1), :], 0.0), axis=1, keepdims=True
+            )
+            value = (2.0 * sums[k] / top - count) * own_scale
+            merged[c * CHUNK + k] = value
+            total = total + value * value
+    ssq[...] = total[0:8] + total[8:16]
+
+    ssq_copies = [
+        remote(
+            ssq, ssq_in.at[i], q_send.at[i], q_recv.at[i], ((me + d) % 16, (core + c) % 2)
+        )
+        for i, (d, c) in enumerate(others)
+    ]
+    for c in ssq_copies:
+        c.start()
+
+    flat = merged[...].reshape(half * 16, BLOCK)
+    hi = flat.astype(jnp.bfloat16)
+    rest = flat - hi.astype(jnp.float32)
+    mid = rest.astype(jnp.bfloat16)
+    lo = (rest - mid.astype(jnp.float32)).astype(jnp.bfloat16)
+    restored = (
+        jnp.dot(hi, hb, preferred_element_type=jnp.float32)
+        + jnp.dot(mid, hb, preferred_element_type=jnp.float32)
+        + jnp.dot(lo, hb, preferred_element_type=jnp.float32)
+    ) * inv_root
+    merged[...] = restored.reshape(half, 16, BLOCK)
+
+    for c in ssq_copies:
+        c.wait_recv()
+    squares = jnp.sum(ssq[...] + jnp.sum(ssq_in[...], axis=0), keepdims=True)
+    root_mean = jnp.sqrt(squares / entries + epsilon)
+    factor = clip[0] / jnp.maximum(root_mean, clip[0])
+
+    def piece(zz, yy, xx):
+        return out.at[
+            pl.ds(pl.multiple_of(16 * (2 * zz + yy), 16), 16),
+            pl.ds(pl.multiple_of(xx * (half * BLOCK), BLOCK), half * BLOCK),
+        ]
+
+    for k in range(half):
+        b = x * half + k
+        out[
+            pl.ds(pl.multiple_of(16 * group, 16), 16),
+            pl.ds(pl.multiple_of(b * BLOCK, BLOCK), BLOCK),
+        ] = (merged[k] * flip[pl.ds(b, 1), :] * factor).astype(jnp.bfloat16)
+
+    own = piece(z, y, x)
+    sent = []
+
+    def go(copy):
+        copy.start()
+        sent.append(copy)
+
+    for d in range(1, 4):
+        go(remote(own, own, g_send.at[d - 1, 0], z_recv.at[d - 1], dev(z_peer(d), mine)))
+    for s in range(4):
+        zs = (z + 4 - s) % 4
+        here = piece(zs, y, x)
+        if s:
+            remote(here, here, g_send.at[s - 1, 0], z_recv.at[s - 1], dev(z, mine)).wait_recv()
+        for d in range(1, 4):
+            go(remote(here, here, g_send.at[s, d], p_recv.at[s, d - 1], dev(z, plane_peer(d))))
+    for s in range(4):
+        zs = (z + 4 - s) % 4
+        for d in range(1, 4):
+            dx, dy = d % 2, d // 2
+            there = piece(zs, (y + dy) % 2, (x + dx) % 2)
+            remote(there, there, g_send.at[s, d], p_recv.at[s, d - 1], dev(z, plane_peer(d))).wait_recv()
+
+    for c in range(chunks):
+        for d in range(1, 4):
+            plane_copy(c, d).wait_send()
+            z_copy(c, d).wait_send()
+    for c in ssq_copies:
+        c.wait_send()
+    for c in sent:
+        c.wait_send()
+
+
+def fused_body(gradient, thresholds, sign_bits, levels, clip_rms):
+    rows, columns = gradient.shape[1], gradient.shape[2]
+    blocks = columns // BLOCK
+    half = blocks // 2
+    chunks = half // CHUNK
+    flip = (1 - 2 * sign_bits).astype(jnp.float32).reshape(blocks, BLOCK)
+    entries = float(rows * lax.axis_size("tensor") * columns)
+    vmem = pl.BlockSpec(memory_space=pltpu.VMEM)
+    smem = pl.BlockSpec(memory_space=pltpu.SMEM)
+    f32 = jnp.float32
+    padded = -(-blocks // 8) * 8
+    dma = pltpu.SemaphoreType.DMA
+    return pl.pallas_call(
+        functools.partial(kernel, entries),
+        out_shape=jax.ShapeDtypeStruct((rows, columns), jnp.bfloat16),
+        in_specs=[vmem, vmem, vmem, vmem, smem, smem],
+        out_specs=vmem,
+        scratch_shapes=[
+            pltpu.VMEM((blocks, rows, BLOCK), f32),
+            pltpu.VMEM((blocks, rows, BLOCK), f32),
+            pltpu.VMEM((padded, BLOCK), f32),
+            pltpu.VMEM((3, padded, BLOCK), f32),
+            pltpu.VMEM((3, padded, BLOCK), f32),
+            pltpu.VMEM((chunks, 4, 4, CHUNK, 16, BLOCK), f32),
+            pltpu.VMEM((chunks, 3, 4, CHUNK, 16, BLOCK), f32),
+            pltpu.VMEM((chunks, 4, CHUNK, 16, BLOCK), f32),
+            pltpu.VMEM((chunks, 3, CHUNK, 16, BLOCK), f32),
+            pltpu.VMEM((half, 16, BLOCK), f32),
+            pltpu.VMEM((8, BLOCK), f32),
+            pltpu.VMEM((31, 8, BLOCK), f32),
+            dma((6,)), dma((3,)), dma((3,)),
+            dma((chunks, 3)), dma((chunks, 3)), dma((chunks, 3)), dma((chunks, 3)),
+            dma((31,)), dma((31,)),
+            dma((4, 4)), dma((3,)), dma((4, 3)),
+        ],
+        compiler_params=pltpu.CompilerParams(
+            collective_id=0, has_side_effects=True, vmem_limit_bytes=40 * 1024 * 1024
+        ),
+    )(gradient[0], thresholds[0], flip, hadamard_matrix(BLOCK), levels, clip_rms)
 
 
 def encode_units(normed, dither, table, units):
@@ -96,4 +384,6 @@
 def solution(mesh):
     in_specs = (P("dp", "tensor", None), P("dp", "tensor", None), P(), P(), P())
     out_specs = P("tensor", None)
-    return jax.shard_map(body, mesh=mesh, in_specs=in_specs, out_specs=out_specs, check_vma=False)
+    sixteen = mesh.shape["dp"] == 16 and mesh.shape["tensor"] == 2
+    call = fused_body if sixteen else body
+    return jax.shard_map(call, mesh=mesh, in_specs=in_specs, out_specs=out_specs, check_vma=False)

time: 307 us -> 68.5 us (0.22)
  blocking collectives: 160 us -> 0 us
  waiting for transfers between devices: 75.2 us -> 0 us
  Pallas kernels: 0 us -> 62.3 us
  other arithmetic: 31.4 us -> 0.94 us
  local copies, waits for them, and re-layouts: 19 us -> 4.25 us
  between operations: 14.9 us -> 0.7 us
  matrix products: 5.2 us -> 0 us
    pmax x1 -> x0, blocking collectives: 78.6 us -> none  [body(): block_scale = lax.pmax(local_peak, 'dp') + epsilon]
    unnamed x2 -> x0, waiting for transfers between devices: 75.2 us -> none
    pallas_call x0 -> x1, Pallas kernels: none -> 62.3 us  [fused_body(): pl.pallas_call(functools.partial(kernel, entries), out_shape=jax.ShapeDty...]
    all_gather x1 -> x0, blocking collectives: 44.7 us -> none  [body(): gathered = lax.all_gather(owned_part, 'dp', axis=0, tiled=True)]
    psum x1 -> x0, blocking collectives: 37.1 us -> none  [body(): squares = lax.psum(jnp.sum(restored * restored), ('dp', 'tensor'))]
    add x2 -> x0, other arithmetic: 27.6 us -> none  [the longest x1 27.6 us: encode_units(): return low_unit + (high_unit - low_unit) * ramp]
    div x4 -> x0, local copies, waits for them, and re-layouts: 8.55 us -> none  [the longest x2 5.4 us: body(): (thresholds[0].reshape(row_count * block_count, BLOCK).astype(jnp.float32...]
    dot_general x3 -> x0, matrix products: 5.2 us -> none  [the longest x1 3.3 us: body(): jnp.dot(blocks, hadamard.astype(jnp.bfloat16), preferred_element_type=jnp...]
  transfers between devices with their start and end apart: 1 -> 0, of which waited for: 1 -> 0; matrix products, arithmetic and copies ran while one was open for 0% -> 0% of each run, Pallas kernels for 0% -> 0%
where the time goes in v1:
time: 68.5 us; the launch traced here: 68.2 us
  Pallas kernels  62.3 us (91%)
  local copies, waits for them, and re-layouts  4.25 us (6%)
  other arithmetic  0.94 us (1%)
  between operations  0.7 us (1%)
    pallas_call x1, Pallas kernels, fused_body(): pl.pallas_call(functools.partial(kernel, entries), out_shape=jax.ShapeDty...  62.3 us
    unnamed x7, local copies, waits for them, and re-layouts  4.25 us

profile of v1, /device:TPU:0, one launch (start us, length us, event | category | flops | bytes accessed | tf_op | source)
XLA Modules:
  0.0 68.2 jit_solution(8609400585045057821)
XLA Ops:
  0.7 0.7 %convert_bitcast_fusion.flip = f32[28,128]{1,0:T(8,128)S(1)} fusion(s32[3584]{0:T(1024)} %param.7), kind=kLoop, calls=%fused_computation.7 | loop fusion | flops 10752 | bytes 28672 | tf_op jit(solution)/shard_map/reshape | solution.py:278
  1.4 0.2 fusion.3.had
  1.6 0.0 copy-start
  1.6 1.5 %copy-done = s32[1,128,3584]{2,1,0:T(8,128)S(1)} copy-done((s32[1,128,3584]{2,1,0:T(8,128)S(1)}, s32[1,128,3584]{2,1,0:T(8,128)}, u32[]{:S(2)}) %copy-start) | copy-done | bytes 1835032
  3.1 0.0 copy-start.1
  3.1 1.2 %copy-done.1 = bf16[1,128,3584]{2,1,0:T(8,128)(2,1)S(1)} copy-done((bf16[1,128,3584]{2,1,0:T(8,128)(2,1)S(1)}, bf16[1,128,3584]{2,1,0:T(8,128)(2,1)}, u32[]{:S(2)}) %copy-start.1) | copy-done | bytes 917528
  4.3 0.0 copy-start.2
  4.3 0.7 copy-done.2
  5.0 62.3 %shard_map.55 = bf16[128,3584]{1,0:T(8,128)(2,1)S(1)} custom-call(bf16[128,3584]{1,0:T(8,128)(2,1)S(1)} %bitcast.5, s32[128,3584]{1,0:T(8,128)S(1)} %bitcast.4, f32[28,128]{1,0:T(8,128)S(1)} %convert_bitcast_fusion.flip, f32[128,128]{1,0:T(8,128)S(1)} %fusion.3.had, s32[16]{0:T(128)S(1)} %copy-done.2, f32[1]{0:T(128)S(6)} %copy.7.clip), custom_call_target="tpu_custom_call" | custom-call | tf_op jit(solution)/shard_map/pallas_call | solution.py:285
  67.3 0.9 %copy.8 = bf16[128,3584]{1,0:T(8,128)(2,1)} copy(bf16[128,3584]{1,0:T(8,128)(2,1)S(1)} %shard_map.55) | data formatting | bytes 1835008
  (4 shorter events, 0.0 us)
Async XLA Ops:
  1.6 1.5 %copy-start = (s32[1,128,3584]{2,1,0:T(8,128)S(1)}, s32[1,128,3584]{2,1,0:T(8,128)}, u32[]{:S(2)}) copy-start(s32[1,128,3584]{2,1,0:T(8,128)} %param.6) | copy-start | bytes 5505028
  3.1 1.2 %copy-start.1 = (bf16[1,128,3584]{2,1,0:T(8,128)(2,1)S(1)}, bf16[1,128,3584]{2,1,0:T(8,128)(2,1)}, u32[]{:S(2)}) copy-start(bf16[1,128,3584]{2,1,0:T(8,128)(2,1)} %param.5) | copy-start | bytes 2752516
  4.3 0.7 copy-start.2

commit v2 on v1

--- a/solution.py
+++ b/solution.py
@@ -10,6 +10,8 @@
 
 BLOCK = 128
 MESH = pl.DeviceIdType.MESH
+LOADS = 4
+GUARD = 64
 CHUNK = 2
 epsilon = 1e-06
 sharpness = 16.0
@@ -28,7 +30,8 @@
 
 
 def kernel(
-    entries, grad, thr, flip, had, levels, clip, out,
+    entries, grad_in, thr_in, sign_in, levels, clip, out,
+    grad, thr, sign, flip, load,
     rot, amp, peak, peak_a, peak_b, send, recv_a, part, recv_b, merged, ssq, ssq_in,
     pk_send, pk_a, pk_b, a_send, a_recv, b_send, b_recv, q_send, q_recv, g_send, z_recv, p_recv,
 ):
@@ -58,13 +61,37 @@
     mine = y * 2 + x
     others = [(d, c) for d in range(16) for c in range(2) if (d, c) != (0, 0)]
 
+    fetch_sign = pltpu.make_async_copy(sign_in, sign, load.at[0])
+    fetch_sign.start()
+    quarter = grad.shape[1] // LOADS
+    fetch_grad = [
+        pltpu.make_async_copy(
+            grad_in.at[0, :, pl.ds(i * quarter, quarter)],
+            grad.at[:, pl.ds(i * quarter, quarter)],
+            load.at[i + 2],
+        )
+        for i in range(LOADS)
+    ]
+    for c in fetch_grad:
+        c.start()
+    fetch_thr = pltpu.make_async_copy(thr_in.at[0], thr, load.at[1])
+    fetch_thr.start()
+
     barrier = pltpu.get_barrier_semaphore()
     for d, c in others:
         pl.semaphore_signal(
             barrier, inc=1, device_id=((me + d) % 16, (core + c) % 2), device_id_type=MESH
         )
 
-    hb = had[...].astype(jnp.bfloat16)
+    lane = lax.broadcasted_iota(jnp.int32, (BLOCK, BLOCK), 1)
+    row = lax.broadcasted_iota(jnp.int32, (BLOCK, BLOCK), 0)
+    bits = lane & row
+    bits = bits ^ (bits >> 4)
+    bits = bits ^ (bits >> 2)
+    bits = bits ^ (bits >> 1)
+    hb = (1 - 2 * (bits & 1)).astype(jnp.float32).astype(jnp.bfloat16)
+    fetch_sign.wait()
+    flip[...] = (1 - 2 * sign[...]).astype(jnp.float32)
     peak[...] = jnp.zeros_like(peak)
 
     def rotate(b, _):
@@ -77,7 +104,9 @@
         peak[pl.ds(b, 1), :] = jnp.max(jnp.abs(turned), axis=0, keepdims=True) * inv_root
         return 0
 
-    lax.fori_loop(0, blocks, rotate, 0)
+    for i in range(LOADS):
+        fetch_grad[i].wait()
+        lax.fori_loop(i * blocks // LOADS, (i + 1) * blocks // LOADS, rotate, 0)
 
     def amplitude(b, _):
         cols = pl.ds(pl.multiple_of(b * BLOCK, BLOCK), BLOCK)
@@ -94,6 +123,7 @@
     ]
     for c in first:
         c.start()
+    fetch_thr.wait()
     lax.fori_loop(0, half, amplitude, 0)
     for c in first:
         c.wait()
@@ -119,9 +149,9 @@
     peak_a[0] = scale
     peak_a[1] = (half_top * inv_root) / scale
 
-    lane = lax.broadcasted_iota(jnp.int32, (BLOCK, BLOCK), 1)
-    row = lax.broadcasted_iota(jnp.int32, (BLOCK, BLOCK), 0)
     decay = math.exp(-sharpness)
+    step = (2.0**20 - 2.0 * GUARD) / top
+    shift = 2.0 * GUARD * count / (2.0**20 - 2.0 * GUARD) + count
 
     def code_of(b):
         inverse = jnp.sum(
@@ -154,11 +184,17 @@
     def encode_chunk(c):
         for h in range(2):
             def one(k, _):
-                code = code_of(h * half + c * CHUNK + k)
-                for zz in range(4):
-                    for yy in range(2):
+                number = (code_of(h * half + c * CHUNK + k) * step + (GUARD + 0.5)).astype(jnp.int32)
+                number = jnp.clip(number, 0, 2**20 - 1)
+                high = ((number >> 4) - 2**15).astype(jnp.int16)
+                nibble = number & 15
+                for yy in range(2):
+                    four = jnp.full((16, BLOCK), -(2**15), jnp.int32)
+                    for zz in range(4):
                         at = 16 * (2 * zz + yy)
-                        send[c, yy * 2 + h, zz, k] = code[at:at + 16]
+                        send[c, yy * 2 + h, zz, k] = high[at:at + 16]
+                        four = four + (nibble[at:at + 16] << (4 * zz))
+                    send[c, yy * 2 + h, 4, k] = four.astype(jnp.int16)
                 return 0
             lax.fori_loop(0, CHUNK, one, 0)
         for d in range(1, 4):
@@ -167,7 +203,12 @@
     def add_plane(c):
         for d in range(1, 4):
             plane_copy(c, d).wait_recv()
-        part[c] = (send[c, mine] + recv_a[c, 0]) + (recv_a[c, 1] + recv_a[c, 2])
+        sources = [send.at[c, mine], recv_a.at[c, 0], recv_a.at[c, 1], recv_a.at[c, 2]]
+        fours = [ref[4].astype(jnp.int32) + 2**15 for ref in sources]
+        for zz in range(4):
+            upper = sum(ref[zz].astype(jnp.int32) for ref in sources) + 4 * 2**15
+            lower = sum((four >> (4 * zz)) & 15 for four in fours)
+            part[c, zz] = (upper * 16 + lower).astype(jnp.float32)
         for d in range(1, 4):
             z_copy(c, d).start()
 
@@ -192,7 +233,7 @@
             own_scale = jnp.sum(
                 jnp.where(own_rows, peak_a[0, pl.ds(b, 1), :], 0.0), axis=1, keepdims=True
             )
-            value = (2.0 * sums[k] / top - count) * own_scale
+            value = (sums[k] * (2.0 / (step * top)) - shift) * own_scale
             merged[c * CHUNK + k] = value
             total = total + value * value
     ssq[...] = total[0:8] + total[8:16]
@@ -275,26 +316,31 @@
     blocks = columns // BLOCK
     half = blocks // 2
     chunks = half // CHUNK
-    flip = (1 - 2 * sign_bits).astype(jnp.float32).reshape(blocks, BLOCK)
     entries = float(rows * lax.axis_size("tensor") * columns)
     vmem = pl.BlockSpec(memory_space=pltpu.VMEM)
+    hbm = pl.BlockSpec(memory_space=pl.ANY)
     smem = pl.BlockSpec(memory_space=pltpu.SMEM)
     f32 = jnp.float32
     padded = -(-blocks // 8) * 8
     dma = pltpu.SemaphoreType.DMA
     return pl.pallas_call(
         functools.partial(kernel, entries),
-        out_shape=jax.ShapeDtypeStruct((rows, columns), jnp.bfloat16),
-        in_specs=[vmem, vmem, vmem, vmem, smem, smem],
+        out_shape=pltpu.VMEM((rows, columns), jnp.bfloat16),
+        in_specs=[hbm, hbm, hbm, smem, smem],
         out_specs=vmem,
         scratch_shapes=[
+            pltpu.VMEM((rows, columns), jnp.bfloat16),
+            pltpu.VMEM((rows, columns), jnp.int32),
+            pltpu.VMEM((blocks, BLOCK), jnp.int32),
+            pltpu.VMEM((blocks, BLOCK), f32),
+            dma((LOADS + 2,)),
             pltpu.VMEM((blocks, rows, BLOCK), f32),
             pltpu.VMEM((blocks, rows, BLOCK), f32),
             pltpu.VMEM((padded, BLOCK), f32),
             pltpu.VMEM((3, padded, BLOCK), f32),
             pltpu.VMEM((3, padded, BLOCK), f32),
-            pltpu.VMEM((chunks, 4, 4, CHUNK, 16, BLOCK), f32),
-            pltpu.VMEM((chunks, 3, 4, CHUNK, 16, BLOCK), f32),
+            pltpu.VMEM((chunks, 4, 5, CHUNK, 16, BLOCK), jnp.int16),
+            pltpu.VMEM((chunks, 3, 5, CHUNK, 16, BLOCK), jnp.int16),
             pltpu.VMEM((chunks, 4, CHUNK, 16, BLOCK), f32),
             pltpu.VMEM((chunks, 3, CHUNK, 16, BLOCK), f32),
             pltpu.VMEM((half, 16, BLOCK), f32),
@@ -306,9 +352,9 @@
             dma((4, 4)), dma((3,)), dma((4, 3)),
         ],
         compiler_params=pltpu.CompilerParams(
-            collective_id=0, has_side_effects=True, vmem_limit_bytes=40 * 1024 * 1024
+            collective_id=0, has_side_effects=True, vmem_limit_bytes=60 * 1024 * 1024
         ),
-    )(gradient[0], thresholds[0], flip, hadamard_matrix(BLOCK), levels, clip_rms)
+    )(gradient, thresholds, sign_bits.reshape(blocks, BLOCK), levels, clip_rms)
 
 
 def encode_units(normed, dither, table, units):

time: 68.5 us -> 60.1 us (0.88)
  Pallas kernels: 62.3 us -> 58.2 us
  local copies, waits for them, and re-layouts: 4.25 us -> 0.93 us
  other arithmetic: 0.94 us -> 0 us
    pallas_call x1, Pallas kernels: 62.3 us -> 58.2 us  [fused_body(): pl.pallas_call(functools.partial(kernel, entries), out_shape=pltpu.VMEM((...]
    unnamed x7 -> x1, local copies, waits for them, and re-layouts: 4.25 us -> 0.93 us
    reshape x1 -> x0, other arithmetic: 0.72 us -> none  [fused_body(): flip = (1 - 2 * sign_bits).astype(jnp.float32).reshape(blocks, BLOCK)]
where the time goes in v2:
time: 60.1 us; the launch traced here: 59.8 us
  Pallas kernels  58.2 us (97%)
  local copies, waits for them, and re-layouts  0.93 us (2%)
  between operations  0.66 us (1%)
    pallas_call x1, Pallas kernels, fused_body(): pl.pallas_call(functools.partial(kernel, entries), out_shape=pltpu.VMEM((...  58.2 us

profile of v2, /device:TPU:0, one launch (start us, length us, event | category | flops | bytes accessed | tf_op | source)
XLA Modules:
  0.0 59.8 jit_solution(7560407145945428835)
XLA Ops:
  0.7 58.2 %shard_map.55 = bf16[128,3584]{1,0:T(8,128)(2,1)S(1)} custom-call(bf16[1,128,3584]{2,1,0:T(8,128)(2,1)} %grad_in.1, s32[1,128,3584]{2,1,0:T(8,128)} %thr_in.1, s32[28,128]{1,0:T(8,128)} %bitcast.1, s32[16]{0:T(128)} %levels.1, f32[1]{0:T(128)S(6)} %copy.8.clip), custom_call_target="tpu_custom_call" | custom-call | tf_op jit(solution)/shard_map/pallas_call | solution.py:326
  58.9 0.9 %copy.7 = bf16[128,3584]{1,0:T(8,128)(2,1)} copy(bf16[128,3584]{1,0:T(8,128)(2,1)S(1)} %shard_map.55) | data formatting | bytes 1835008

commit v3 on v2

--- a/solution.py
+++ b/solution.py
@@ -106,7 +106,7 @@
 
     for i in range(LOADS):
         fetch_grad[i].wait()
-        lax.fori_loop(i * blocks // LOADS, (i + 1) * blocks // LOADS, rotate, 0)
+        lax.fori_loop(i * blocks // LOADS, (i + 1) * blocks // LOADS, rotate, 0, unroll=True)
 
     def amplitude(b, _):
         cols = pl.ds(pl.multiple_of(b * BLOCK, BLOCK), BLOCK)
@@ -124,7 +124,7 @@
     for c in first:
         c.start()
     fetch_thr.wait()
-    lax.fori_loop(0, half, amplitude, 0)
+    lax.fori_loop(0, half, amplitude, 0, unroll=2)
     for c in first:
         c.wait()
     peak[...] = jnp.maximum(
@@ -136,7 +136,7 @@
     ]
     for c in second:
         c.start()
-    lax.fori_loop(half, blocks, amplitude, 0)
+    lax.fori_loop(half, blocks, amplitude, 0, unroll=2)
     for c in second:
         c.wait()
     scale = (
@@ -196,7 +196,7 @@
                         four = four + (nibble[at:at + 16] << (4 * zz))
                     send[c, yy * 2 + h, 4, k] = four.astype(jnp.int16)
                 return 0
-            lax.fori_loop(0, CHUNK, one, 0)
+            lax.fori_loop(0, CHUNK, one, 0, unroll=True)
         for d in range(1, 4):
             plane_copy(c, d).start()
 

time: 60.1 us -> 57 us (0.948)
  Pallas kernels: 58.2 us -> 55.2 us
    pallas_call x1, Pallas kernels: 58.2 us -> 55.2 us  [fused_body(): pl.pallas_call(functools.partial(kernel, entries), out_shape=pltpu.VMEM((...]
where the time goes in v3:
time: 57 us; the launch traced here: 56.7 us
  Pallas kernels  55.2 us (97%)
  local copies, waits for them, and re-layouts  0.93 us (2%)
  between operations  0.66 us (1%)
    pallas_call x1, Pallas kernels, fused_body(): pl.pallas_call(functools.partial(kernel, entries), out_shape=pltpu.VMEM((...  55.2 us

profile of v3, /device:TPU:0, one launch (start us, length us, event | category | flops | bytes accessed | tf_op | source)
XLA Modules:
  0.0 56.7 jit_solution(2195109631181929527)
XLA Ops:
  0.7 55.2 %shard_map.55 = bf16[128,3584]{1,0:T(8,128)(2,1)S(1)} custom-call(bf16[1,128,3584]{2,1,0:T(8,128)(2,1)} %grad_in.1, s32[1,128,3584]{2,1,0:T(8,128)} %thr_in.1, s32[28,128]{1,0:T(8,128)} %bitcast.1, s32[16]{0:T(128)} %levels.1, f32[1]{0:T(128)S(6)} %copy.8.clip), custom_call_target="tpu_custom_call" | custom-call | tf_op jit(solution)/shard_map/pallas_call | solution.py:326
  55.8 0.9 %copy.7 = bf16[128,3584]{1,0:T(8,128)(2,1)} copy(bf16[128,3584]{1,0:T(8,128)(2,1)S(1)} %shard_map.55) | data formatting | bytes 1835008

commit v4 on v3

--- a/solution.py
+++ b/solution.py
@@ -214,9 +214,9 @@
 
     for c in range(chunks):
         encode_chunk(c)
-        if c >= 2:
-            add_plane(c - 2)
-    for c in range(max(chunks - 2, 0), chunks):
+        if c >= 3:
+            add_plane(c - 3)
+    for c in range(max(chunks - 3, 0), chunks):
         add_plane(c)
 
     group = 2 * z + y

time: 57 us -> 55.3 us (0.970)
  Pallas kernels: 55.2 us -> 53.4 us
    pallas_call x1, Pallas kernels: 55.2 us -> 53.4 us  [fused_body(): pl.pallas_call(functools.partial(kernel, entries), out_shape=pltpu.VMEM((...]
where the time goes in v4:
time: 55.3 us; the launch traced here: 55 us
  Pallas kernels  53.4 us (97%)
  local copies, waits for them, and re-layouts  0.93 us (2%)
  between operations  0.66 us (1%)
    pallas_call x1, Pallas kernels, fused_body(): pl.pallas_call(functools.partial(kernel, entries), out_shape=pltpu.VMEM((...  53.4 us

profile of v4, /device:TPU:0, one launch (start us, length us, event | category | flops | bytes accessed | tf_op | source)
XLA Modules:
  0.0 55.0 jit_solution(15192990845366156774)
XLA Ops:
  0.7 53.4 %shard_map.55 = bf16[128,3584]{1,0:T(8,128)(2,1)S(1)} custom-call(bf16[1,128,3584]{2,1,0:T(8,128)(2,1)} %grad_in.1, s32[1,128,3584]{2,1,0:T(8,128)} %thr_in.1, s32[28,128]{1,0:T(8,128)} %bitcast.1, s32[16]{0:T(128)} %levels.1, f32[1]{0:T(128)S(6)} %copy.8.clip), custom_call_target="tpu_custom_call" | custom-call | tf_op jit(solution)/shard_map/pallas_call | solution.py:326
  54.1 0.9 %copy.7 = bf16[128,3584]{1,0:T(8,128)(2,1)} copy(bf16[128,3584]{1,0:T(8,128)(2,1)S(1)} %shard_map.55) | data formatting | bytes 1835008

commit v5 on v4

--- a/solution.py
+++ b/solution.py
@@ -197,7 +197,7 @@
                     send[c, yy * 2 + h, 4, k] = four.astype(jnp.int16)
                 return 0
             lax.fori_loop(0, CHUNK, one, 0, unroll=True)
-        for d in range(1, 4):
+        for d in (3, 1, 2):
             plane_copy(c, d).start()
 
     def add_plane(c):
@@ -292,7 +292,7 @@
         here = piece(zs, y, x)
         if s:
             remote(here, here, g_send.at[s - 1, 0], z_recv.at[s - 1], dev(z, mine)).wait_recv()
-        for d in range(1, 4):
+        for d in (3, 1, 2):
             go(remote(here, here, g_send.at[s, d], p_recv.at[s, d - 1], dev(z, plane_peer(d))))
     for s in range(4):
         zs = (z + 4 - s) % 4

time: 55.3 us -> 54.4 us (0.984)
  Pallas kernels: 53.4 us -> 52.6 us
    pallas_call x1, Pallas kernels: 53.4 us -> 52.6 us  [fused_body(): pl.pallas_call(functools.partial(kernel, entries), out_shape=pltpu.VMEM((...]
where the time goes in v5:
time: 54.4 us; the launch traced here: 54.2 us
  Pallas kernels  52.6 us (97%)
  local copies, waits for them, and re-layouts  0.93 us (2%)
  between operations  0.66 us (1%)
    pallas_call x1, Pallas kernels, fused_body(): pl.pallas_call(functools.partial(kernel, entries), out_shape=pltpu.VMEM((...  52.6 us

profile of v5, /device:TPU:0, one launch (start us, length us, event | category | flops | bytes accessed | tf_op | source)
XLA Modules:
  0.0 54.2 jit_solution(14338492858906091802)
XLA Ops:
  0.7 52.6 %shard_map.55 = bf16[128,3584]{1,0:T(8,128)(2,1)S(1)} custom-call(bf16[1,128,3584]{2,1,0:T(8,128)(2,1)} %grad_in.1, s32[1,128,3584]{2,1,0:T(8,128)} %thr_in.1, s32[28,128]{1,0:T(8,128)} %bitcast.1, s32[16]{0:T(128)} %levels.1, f32[1]{0:T(128)S(6)} %copy.8.clip), custom_call_target="tpu_custom_call" | custom-call | tf_op jit(solution)/shard_map/pallas_call | solution.py:326
  53.3 0.9 %copy.7 = bf16[128,3584]{1,0:T(8,128)(2,1)} copy(bf16[128,3584]{1,0:T(8,128)(2,1)S(1)} %shard_map.55) | data formatting | bytes 1835008
